TPU v7x, 512 devices: a whole 4x8x8 slice. The times are simulated.
512 devices in a mesh: pair: 32 (over y_lo, z), day: 16 (over y_hi, x, core).
Axes of the slice: x: 4, y: 8 (y_hi: 2, y_lo: 4; y = y_hi * 4 + y_lo), z: 8, core: 2. Of those that a mesh axis runs over, the one named last changes fastest.
Arguments:
- spectra: bfloat16 [32, 2, 2048, 1024], P('day', None, 'pair'), may hold values from -6 to 6
- band_weights: float32 [8, 2048], replicated, may hold values from 0.05 to 1
- pair_stations: int32 [1536, 2], replicated, may hold values from 0 to 1023
- block_live: int32 [512], P(('pair', 'day')), may hold values from 1 to 3, 1152 in all
- windows: int32 [1536, 8, 2], P(('pair', 'day')), may hold values from 0 to 4096, as said below
- observed: bfloat16 [1536, 8, 4096], P(('pair', 'day')), may hold values from -6 to 6
Outputs:
- adjoint: float32 [32, 2, 2048, 1024], P('day', None, 'pair')
Inputs may be any that keep to these rules, and one draw needn't show every extreme that they name: Block b holds pairs b * 3 to b * 3 + 2, and its first block_live[b] pairs are live. windows[p, k, 0] < windows[p, k, 1].
All inputs are finite; a program needn't handle non-finite values.
Results may differ from a plain program's by a relative error of at most 0.0035.
Values sent between devices are 32-bit elements; how exact they have to be, the bound alone decides.
A program may use at most 64 MiB of HBM per device.

v0:
```python
import math
import jax
import jax.numpy as jnp
from jax import lax
from jax.sharding import PartitionSpec as P


def table_block(start, width, lags):
    half = lags // 2
    freqs = jnp.arange(half, dtype=jnp.int32)
    lag_index = start + jnp.arange(width, dtype=jnp.int32)
    phase = freqs[:, None] * lag_index[None, :] % lags
    angle = phase.astype(jnp.float32) * (2.0 * math.pi / lags)
    return jnp.concatenate([jnp.cos(angle), -jnp.sin(angle)], axis=0).astype(jnp.bfloat16)


def one_hot_rows(identity, columns):
    return (identity[:, None] == columns[None, :]).astype(jnp.bfloat16)


def gather_rows(flat_spectra, stations):
    count = stations.shape[0]
    station_count = flat_spectra.shape[1]
    width = math.gcd(count, 512)
    columns = jnp.arange(station_count, dtype=jnp.int32)
    dims = (((1,), (1,)), ((), ()))

    def gather_step(index, buffers):
        start = index * width
        identity = lax.dynamic_slice_in_dim(stations, start, width, 0)
        first_hot = one_hot_rows(identity[:, 0], columns)
        second_hot = one_hot_rows(identity[:, 1], columns)
        first_part = lax.dot_general(
            flat_spectra, first_hot, dims, preferred_element_type=jnp.float32
        ).astype(jnp.bfloat16)
        second_part = lax.dot_general(
            flat_spectra, second_hot, dims, preferred_element_type=jnp.float32
        ).astype(jnp.bfloat16)
        return (
            lax.dynamic_update_slice_in_dim(buffers[0], first_part, start, 1),
            lax.dynamic_update_slice_in_dim(buffers[1], second_part, start, 1),
        )

    empty = jnp.zeros((flat_spectra.shape[0], count), jnp.bfloat16)
    return lax.fori_loop(0, count // width, gather_step, (empty, empty))


def cross_stack(first_rows, second_rows, day_count, freq_count):
    count = first_rows.shape[1]
    first = first_rows.reshape(day_count, 2, freq_count, count).astype(jnp.float32)
    second = second_rows.reshape(day_count, 2, freq_count, count).astype(jnp.float32)
    real_part = jnp.sum(first[:, 0] * second[:, 0] + first[:, 1] * second[:, 1], axis=0)
    imag_part = jnp.sum(first[:, 0] * second[:, 1] - first[:, 1] * second[:, 0], axis=0)
    return jnp.stack([real_part, imag_part]).transpose(0, 2, 1)


def add_to_stations(accum, to_first, to_second, stations):
    count = stations.shape[0]
    station_count = accum.shape[1]
    width = math.gcd(count, 512)
    columns = jnp.arange(station_count, dtype=jnp.int32)

    def add_step(index, total):
        start = index * width
        identity = lax.dynamic_slice_in_dim(stations, start, width, 0)
        hot = jnp.concatenate(
            [one_hot_rows(identity[:, 0], columns), one_hot_rows(identity[:, 1], columns)], axis=0
        )
        terms = jnp.concatenate(
            [
                lax.dynamic_slice_in_dim(to_first, start, width, 1),
                lax.dynamic_slice_in_dim(to_second, start, width, 1),
            ],
            axis=1,
        )
        return total + jnp.dot(
            terms,
            hot.astype(jnp.float32),
            precision=lax.Precision.HIGHEST,
            preferred_element_type=jnp.float32,
        )

    return lax.fori_loop(0, count // width, add_step, accum)


def station_terms(accum, first_rows, second_rows, grads, stations, day_count):
    count = first_rows.shape[1]
    freq_count = grads.shape[2]
    first = first_rows.reshape(day_count, 2, freq_count, count).astype(jnp.float32)
    second = second_rows.reshape(day_count, 2, freq_count, count).astype(jnp.float32)
    turned = grads.transpose(0, 2, 1)
    grad_real = turned[0][None]
    grad_imag = turned[1][None]
    to_first = jnp.stack(
        [
            grad_real * second[:, 0] + grad_imag * second[:, 1],
            grad_real * second[:, 1] - grad_imag * second[:, 0],
        ],
        axis=1,
    ).reshape(-1, count)
    to_second = jnp.stack(
        [
            grad_real * first[:, 0] - grad_imag * first[:, 1],
            grad_real * first[:, 1] + grad_imag * first[:, 0],
        ],
        axis=1,
    ).reshape(-1, count)
    return add_to_stations(accum, to_first, to_second, stations)


def body(spectra, band_weights, pair_stations, block_live, windows, observed):
    n_pair = lax.axis_size("pair")
    n_day = lax.axis_size("day")
    per_block, bands, lags = observed.shape
    half = lags // 2
    day_count = spectra.shape[0]
    freq_count = spectra.shape[2]
    station_count = spectra.shape[3]
    days = day_count * n_day
    ordered = (
        pair_stations.reshape(n_pair, n_day, per_block, 2).transpose(1, 0, 2, 3).reshape(-1, 2)
    )
    flat_spectra = spectra.reshape(-1, station_count)
    first_rows, second_rows = gather_rows(flat_spectra, ordered)
    local_stack = cross_stack(first_rows, second_rows, day_count, freq_count)
    total = lax.psum(local_stack, "day")
    day_share = lax.dynamic_slice_in_dim(
        total, lax.axis_index("day") * (n_pair * per_block), n_pair * per_block, 1
    )
    pair_stack = lax.all_to_all(day_share, "pair", split_axis=1, concat_axis=2, tiled=True)
    weights_full = jnp.concatenate([band_weights, band_weights], axis=1)
    flat_stack = jnp.concatenate([pair_stack[0], pair_stack[1]], axis=1)
    weighted = (
        (flat_stack[:, None, :] * weights_full[None])
        .astype(jnp.bfloat16)
        .reshape(per_block * bands, lags)
    )
    live = jnp.arange(per_block, dtype=jnp.int32) < block_live[0]
    row_live = jnp.repeat(live, bands)
    lower_lag = windows[:, :, 0].reshape(-1)
    upper_lag = windows[:, :, 1].reshape(-1)
    observed_rows = observed.reshape(per_block * bands, lags)
    width = min(256, lags)
    forward_scale = 2.0 / math.sqrt(lags * days)
    adjoint_scale = 1.0 / math.sqrt(lags)

    def lag_step(index, accum):
        start = index * width
        block_table = table_block(start, width, lags)
        corr = forward_scale * jnp.dot(weighted, block_table, preferred_element_type=jnp.float32)
        lag_index = start + jnp.arange(width, dtype=jnp.int32)
        inside = (
            row_live[:, None]
            & (lag_index[None, :] >= lower_lag[:, None])
            & (lag_index[None, :] < upper_lag[:, None])
        )
        target = lax.dynamic_slice_in_dim(observed_rows, start, width, 1).astype(jnp.float32)
        misfit = jnp.where(inside, corr - target, 0.0).astype(jnp.bfloat16)
        return accum + lax.dot_general(
            misfit, block_table, (((1,), (1,)), ((), ())), preferred_element_type=jnp.float32
        )

    adjoint_rows = lax.fori_loop(
        0, lags // width, lag_step, jnp.zeros((per_block * bands, lags), jnp.float32)
    )
    summed = jnp.sum(adjoint_rows.reshape(per_block, bands, lags) * weights_full[None], axis=1)
    adjoint_spec = adjoint_scale * summed
    adjoint_split = adjoint_spec.reshape(per_block, 2, half).transpose(1, 0, 2)
    spread = lax.all_to_all(adjoint_split, "pair", split_axis=2, concat_axis=1, tiled=True)
    start_total = jnp.zeros((flat_spectra.shape[0], station_count), jnp.float32)
    all_pairs = lax.all_gather(spread, "day", axis=1, tiled=True)
    flat_out = station_terms(start_total, first_rows, second_rows, all_pairs, ordered, day_count)
    return flat_out.reshape(spectra.shape)


def solution(mesh):
    in_specs = (
        P("day", None, "pair", None),
        P(),
        P(),
        P(("pair", "day")),
        P(("pair", "day"), None, None),
        P(("pair", "day"), None, None),
    )
    out_specs = P("day", None, "pair", None)
    return jax.shard_map(body, mesh=mesh, in_specs=in_specs, out_specs=out_specs, check_vma=False)
```

profile of v0, /device:TPU:1, one launch (start us, length us, event | category | flops | bytes accessed | tf_op | source)
XLA Modules:
  0.0 495.4 jit_solution(16453960934737975883)
XLA Ops:
  8.3 4.5 while.49
  16.7 188.6 %all-reduce.2.cloned.1.call-done = f32[2,1536,64]{1,2,0:T(8,128)} async-done(((f32[2,1536,64]{1,2,0:T(8,128)}), f32[2,1536,64]{1,2,0:T(8,128)}) %all-reduce.2.cloned.1.call-update) | async-done | bytes 786448 | tf_op jit(solution)/shard_map/psum | solution.py:126
  207.2 7.7 %all-to-all-start = ((f32[32,1,384]{2,1,0:T(1,128)}), f32[32,1,384]{2,1,0:T(1,128)S(1)}, u32[]{:S(2)}, u32[]{:S(2)}) async-start(f32[32,1,384]{2,1,0:T(1,128)} %reshape.72), calls=%async_computation | async-start | bytes 98304 | tf_op jit(solution)/shard_map/all_to_all | solution.py:130
  214.9 9.1 %all-to-all-done = f32[32,1,384]{2,1,0:T(1,128)S(1)} async-done(((f32[32,1,384]{2,1,0:T(1,128)}), f32[32,1,384]{2,1,0:T(1,128)S(1)}, u32[]{:S(2)}, u32[]{:S(2)}) %all-to-all-start) | async-done | bytes 49184 | tf_op jit(solution)/shard_map/all_to_all | solution.py:130
  225.7 176.8 %while.51 = (s32[]{:T(128)}, f32[24,4096]{1,0:T(8,128)S(1)}, s32[3,8,1]{1,0,2:T(4,128)}, s32[3,8,1]{1,0,2:T(4,128)}, bf16[24,4096]{1,0:T(8,128)(2,1)}, /*index=5...) while((s32[]{:T(128)}, f32[24,4096]{1,0:T(8,128)S(1)}, ...), condition=%wide.wide.region_6.7_spmd.clone, body=%wide.wide.region_5.6_spmd.clone.sunk | while | flops 118413576 | bytes 7291664 | solution.py:163
  225.8 8.6 %cosine_convert_fusion.3 = (bf16[2048,256]{1,0:T(8,128)(2,1)S(1)}, bf16[2048,256]{1,0:T(8,128)(2,1)S(1)}) fusion(s32[256]{0:T(256)S(1)} %iota_add_fusion.3), kind=kLoop, calls=%fused_computation.26.clone.clone.1 | loop fusion | flops 8912896 | bytes 2098176 | tf_op jit(solution)/shard_map/convert.1
  236.8 8.6 %cosine_convert_fusion.3 = (bf16[2048,256]{1,0:T(8,128)(2,1)S(1)}, bf16[2048,256]{1,0:T(8,128)(2,1)S(1)}) fusion(s32[256]{0:T(256)S(1)} %iota_add_fusion.3), kind=kLoop, calls=%fused_computation.26.clone.clone.1 | loop fusion | flops 8912896 | bytes 2098176 | tf_op jit(solution)/shard_map/convert.1
  247.9 8.6 %cosine_convert_fusion.3 = (bf16[2048,256]{1,0:T(8,128)(2,1)S(1)}, bf16[2048,256]{1,0:T(8,128)(2,1)S(1)}) fusion(s32[256]{0:T(256)S(1)} %iota_add_fusion.3), kind=kLoop, calls=%fused_computation.26.clone.clone.1 | loop fusion | flops 8912896 | bytes 2098176 | tf_op jit(solution)/shard_map/convert.1
  256.7 2.2 convolution_add_fusion.3
  258.9 8.6 %cosine_convert_fusion.3 = (bf16[2048,256]{1,0:T(8,128)(2,1)S(1)}, bf16[2048,256]{1,0:T(8,128)(2,1)S(1)}) fusion(s32[256]{0:T(256)S(1)} %iota_add_fusion.3), kind=kLoop, calls=%fused_computation.26.clone.clone.1 | loop fusion | flops 8912896 | bytes 2098176 | tf_op jit(solution)/shard_map/convert.1
  270.0 8.6 %cosine_convert_fusion.3 = (bf16[2048,256]{1,0:T(8,128)(2,1)S(1)}, bf16[2048,256]{1,0:T(8,128)(2,1)S(1)}) fusion(s32[256]{0:T(256)S(1)} %iota_add_fusion.3), kind=kLoop, calls=%fused_computation.26.clone.clone.1 | loop fusion | flops 8912896 | bytes 2098176 | tf_op jit(solution)/shard_map/convert.1
  281.0 8.6 %cosine_convert_fusion.3 = (bf16[2048,256]{1,0:T(8,128)(2,1)S(1)}, bf16[2048,256]{1,0:T(8,128)(2,1)S(1)}) fusion(s32[256]{0:T(256)S(1)} %iota_add_fusion.3), kind=kLoop, calls=%fused_computation.26.clone.clone.1 | loop fusion | flops 8912896 | bytes 2098176 | tf_op jit(solution)/shard_map/convert.1
  289.8 2.2 convolution_add_fusion.3
  292.1 8.6 %cosine_convert_fusion.3 = (bf16[2048,256]{1,0:T(8,128)(2,1)S(1)}, bf16[2048,256]{1,0:T(8,128)(2,1)S(1)}) fusion(s32[256]{0:T(256)S(1)} %iota_add_fusion.3), kind=kLoop, calls=%fused_computation.26.clone.clone.1 | loop fusion | flops 8912896 | bytes 2098176 | tf_op jit(solution)/shard_map/convert.1
  303.1 8.6 %cosine_convert_fusion.3 = (bf16[2048,256]{1,0:T(8,128)(2,1)S(1)}, bf16[2048,256]{1,0:T(8,128)(2,1)S(1)}) fusion(s32[256]{0:T(256)S(1)} %iota_add_fusion.3), kind=kLoop, calls=%fused_computation.26.clone.clone.1 | loop fusion | flops 8912896 | bytes 2098176 | tf_op jit(solution)/shard_map/convert.1
  314.2 8.6 %cosine_convert_fusion.3 = (bf16[2048,256]{1,0:T(8,128)(2,1)S(1)}, bf16[2048,256]{1,0:T(8,128)(2,1)S(1)}) fusion(s32[256]{0:T(256)S(1)} %iota_add_fusion.3), kind=kLoop, calls=%fused_computation.26.clone.clone.1 | loop fusion | flops 8912896 | bytes 2098176 | tf_op jit(solution)/shard_map/convert.1
  323.0 2.2 convolution_add_fusion.3
  325.2 8.6 %cosine_convert_fusion.3 = (bf16[2048,256]{1,0:T(8,128)(2,1)S(1)}, bf16[2048,256]{1,0:T(8,128)(2,1)S(1)}) fusion(s32[256]{0:T(256)S(1)} %iota_add_fusion.3), kind=kLoop, calls=%fused_computation.26.clone.clone.1 | loop fusion | flops 8912896 | bytes 2098176 | tf_op jit(solution)/shard_map/convert.1
  336.3 8.6 %cosine_convert_fusion.3 = (bf16[2048,256]{1,0:T(8,128)(2,1)S(1)}, bf16[2048,256]{1,0:T(8,128)(2,1)S(1)}) fusion(s32[256]{0:T(256)S(1)} %iota_add_fusion.3), kind=kLoop, calls=%fused_computation.26.clone.clone.1 | loop fusion | flops 8912896 | bytes 2098176 | tf_op jit(solution)/shard_map/convert.1
  347.3 8.6 %cosine_convert_fusion.3 = (bf16[2048,256]{1,0:T(8,128)(2,1)S(1)}, bf16[2048,256]{1,0:T(8,128)(2,1)S(1)}) fusion(s32[256]{0:T(256)S(1)} %iota_add_fusion.3), kind=kLoop, calls=%fused_computation.26.clone.clone.1 | loop fusion | flops 8912896 | bytes 2098176 | tf_op jit(solution)/shard_map/convert.1
  356.1 2.2 convolution_add_fusion.3
  358.4 8.6 %cosine_convert_fusion.3 = (bf16[2048,256]{1,0:T(8,128)(2,1)S(1)}, bf16[2048,256]{1,0:T(8,128)(2,1)S(1)}) fusion(s32[256]{0:T(256)S(1)} %iota_add_fusion.3), kind=kLoop, calls=%fused_computation.26.clone.clone.1 | loop fusion | flops 8912896 | bytes 2098176 | tf_op jit(solution)/shard_map/convert.1
  369.4 8.6 %cosine_convert_fusion.3 = (bf16[2048,256]{1,0:T(8,128)(2,1)S(1)}, bf16[2048,256]{1,0:T(8,128)(2,1)S(1)}) fusion(s32[256]{0:T(256)S(1)} %iota_add_fusion.3), kind=kLoop, calls=%fused_computation.26.clone.clone.1 | loop fusion | flops 8912896 | bytes 2098176 | tf_op jit(solution)/shard_map/convert.1
  380.5 8.6 %cosine_convert_fusion.3 = (bf16[2048,256]{1,0:T(8,128)(2,1)S(1)}, bf16[2048,256]{1,0:T(8,128)(2,1)S(1)}) fusion(s32[256]{0:T(256)S(1)} %iota_add_fusion.3), kind=kLoop, calls=%fused_computation.26.clone.clone.1 | loop fusion | flops 8912896 | bytes 2098176 | tf_op jit(solution)/shard_map/convert.1
  389.3 2.2 convolution_add_fusion.3
  391.5 8.6 %cosine_convert_fusion.3 = (bf16[2048,256]{1,0:T(8,128)(2,1)S(1)}, bf16[2048,256]{1,0:T(8,128)(2,1)S(1)}) fusion(s32[256]{0:T(256)S(1)} %iota_add_fusion.3), kind=kLoop, calls=%fused_computation.26.clone.clone.1 | loop fusion | flops 8912896 | bytes 2098176 | tf_op jit(solution)/shard_map/convert.1
  403.9 3.6 reshape.74
  407.5 3.9 all-to-all-start.1
  411.4 9.1 %all-to-all-done.1 = f32[32,1,384]{2,1,0:T(1,128)S(1)} async-done(((f32[32,1,384]{2,1,0:T(1,128)}), f32[32,1,384]{2,1,0:T(1,128)S(1)}, u32[]{:S(2)}, u32[]{:S(2)}) %all-to-all-start.1) | async-done | bytes 49184 | tf_op jit(solution)/shard_map/all_to_all | solution.py:169
  421.2 3.1 reshape.75
  425.5 39.5 %all_gather.3 = f32[2,1536,64]{2,0,1:T(2,128)S(1)} all-gather(f32[2,96,64]{2,0,1:T(2,128)S(1)} %bitcast.109), channel_id=1, replica_groups=mesh['pair'=32,'day'=16] {'day'}, dimensions={1}, use_global_device_ids=true | all-gather | bytes 835584 | tf_op jit(solution)/shard_map/all_gather | solution.py:171
  475.0 12.5 %while.50 = (s32[]{:T(128)}, f32[256,1024]{1,0:T(8,128)S(1)}, f32[256,1536]{1,0:T(8,128)}, f32[256,1536]{1,0:T(8,128)}, s32[1536,2]{0,1:T(2,128)S(1)}, /*index=5...) while((s32[]{:T(128)}, f32[256,1024]{1,0:T(8,128)S(1)}, f32[256,1536]{1,0:T(8,128)}, ...), condition=%wide.region_9.10_spmd.clone.clone, body=%wide.region_8.9_spmd.clone.clone.sunk | while | flops 3224109056 | bytes 7352501 | solution.py:83
  (156 shorter events, 66.6 us)
Async XLA Ops:
  6.5 1.8 copy-start.8
  6.5 198.8 %all-reduce.2.cloned.1.call-start = ((), (), s32[]{:S(2)}) async-start(), calls=%async_computation.2 | async-start | bytes 1572864 | tf_op jit(solution)/shard_map/psum | solution.py:126
  13.2 1.1 copy-start
  13.2 1.6 copy-start.2
  14.8 1.0 copy-start.7
  14.8 1.8 copy-start.4
  15.8 209.9 %copy-start.5 = (s32[3,8,1]{1,0,2:T(4,128)}, s32[3,8,1]{1,0,2:T(4,128)S(1)}, u32[]{:S(2)}) copy-start(s32[3,8,1]{1,0,2:T(4,128)S(1)} %copy.75) | copy-start | bytes 292
  15.9 209.8 %copy-start.6 = (s32[3,8,1]{1,0,2:T(4,128)}, s32[3,8,1]{1,0,2:T(4,128)S(1)}, u32[]{:S(2)}) copy-start(s32[3,8,1]{1,0,2:T(4,128)S(1)} %copy.76) | copy-start | bytes 292
  207.2 16.8 %all-to-all-start = ((f32[32,1,384]{2,1,0:T(1,128)}), f32[32,1,384]{2,1,0:T(1,128)S(1)}, u32[]{:S(2)}, u32[]{:S(2)}) async-start(f32[32,1,384]{2,1,0:T(1,128)} %reshape.72), calls=%async_computation | async-start | bytes 98304 | tf_op jit(solution)/shard_map/all_to_all | solution.py:130
  407.5 13.0 %all-to-all-start.1 = ((f32[32,1,384]{2,1,0:T(1,128)}), f32[32,1,384]{2,1,0:T(1,128)S(1)}, u32[]{:S(2)}, u32[]{:S(2)}) async-start(f32[32,1,384]{2,1,0:T(1,128)} %reshape.74), calls=%async_computation.1 | async-start | bytes 98304 | tf_op jit(solution)/shard_map/all_to_all | solution.py:169
  464.9 5.7 %copy-start.1 = (f32[2,2,64,1536]{3,2,1,0:T(8,128)S(1)}, f32[2,2,64,1536]{3,2,1,0:T(8,128)}, u32[]{:S(2)}) copy-start(f32[2,2,64,1536]{3,2,1,0:T(8,128)} %copy-done) | copy-start | bytes 4718596
  464.9 5.7 %copy-start.3 = (f32[2,2,64,1536]{3,2,1,0:T(8,128)S(1)}, f32[2,2,64,1536]{3,2,1,0:T(8,128)}, u32[]{:S(2)}) copy-start(f32[2,2,64,1536]{3,2,1,0:T(8,128)} %copy-done.2) | copy-start | bytes 4718596
  473.3 1.7 copy-start.9
  487.6 1.0 copy-start.10
Sparse Core Ops, SparseCore 0:
  15.9 189.3 all-reduce.1
where the time goes:
time: 497 us; the launch traced here: 495 us
  waiting for transfers between devices  207 us (42%)
  other arithmetic  148 us (30%)
  matrix products  45 us (9%)
  blocking collectives  39.5 us (8%)
  local copies, waits for them, and re-layouts  29.9 us (6%)
  between operations  14.4 us (3%)
  starting transfers between devices  11.5 us (2%)
    psum x1, waiting for transfers between devices, body(): total = lax.psum(local_stack, 'day')  189 us
    another operation x16, other arithmetic  138 us
    all_gather x1, blocking collectives, body(): all_pairs = lax.all_gather(spread, 'day', axis=1, tiled=True)  39.5 us
    dot_general x16, matrix products, lag_step(): lax.dot_general(misfit, block_table, (((1,), (1,)), ((), ())), preferred_...  35.5 us
    unnamed x29, local copies, waits for them, and re-layouts  10.3 us
  transfers between devices with their start and end apart: 3, of which 3 were waited for; matrix products, arithmetic and copies ran while one was open for 0% of the time, Pallas kernels for 0%

commit v1 on v0

--- a/solution.py
+++ b/solution.py
@@ -123,7 +123,7 @@
     flat_spectra = spectra.reshape(-1, station_count)
     first_rows, second_rows = gather_rows(flat_spectra, ordered)
     local_stack = cross_stack(first_rows, second_rows, day_count, freq_count)
-    total = lax.psum(local_stack, "day")
+    total = jnp.sum(lax.all_gather(local_stack, "day"), axis=0)
     day_share = lax.dynamic_slice_in_dim(
         total, lax.axis_index("day") * (n_pair * per_block), n_pair * per_block, 1
     )

time: 497 us -> 460 us (0.926)
  waiting for transfers between devices: 207 us -> 169 us
  blocking collectives: 39.5 us -> 33.4 us
  other arithmetic: 148 us -> 154 us
    psum x1 -> x0, waiting for transfers between devices: 189 us -> none  [body(): total = lax.psum(local_stack, 'day')]
    all_gather x0 -> x1, waiting for transfers between devices: none -> 151 us  [body(): total = jnp.sum(lax.all_gather(local_stack, 'day'), axis=0)]
    all_gather x1, blocking collectives: 39.5 us -> 33.4 us  [body(): all_pairs = lax.all_gather(spread, 'day', axis=1, tiled=True)]
    reduce_sum x0 -> x1, other arithmetic: none -> 5.85 us  [body(): total = jnp.sum(lax.all_gather(local_stack, 'day'), axis=0)]
where the time goes in v1:
time: 460 us; the launch traced here: 457 us
  waiting for transfers between devices  169 us (37%)
  other arithmetic  154 us (33%)
  matrix products  45 us (10%)
  blocking collectives  33.4 us (7%)
  local copies, waits for them, and re-layouts  29 us (6%)
  between operations  14.4 us (3%)
  starting transfers between devices  11.5 us (2%)
    all_gather x1, waiting for transfers between devices, body(): total = jnp.sum(lax.all_gather(local_stack, 'day'), axis=0)  151 us
    another operation x16, other arithmetic  138 us
    dot_general x16, matrix products, lag_step(): lax.dot_general(misfit, block_table, (((1,), (1,)), ((), ())), preferred_...  35.5 us
    all_gather x1, blocking collectives, body(): all_pairs = lax.all_gather(spread, 'day', axis=1, tiled=True)  33.4 us
    unnamed x29, local copies, waits for them, and re-layouts  10.3 us
  transfers between devices with their start and end apart: 3, of which 3 were waited for; matrix products, arithmetic and copies ran while one was open for 0% of the time, Pallas kernels for 0%

profile of v1, /device:TPU:1, one launch (start us, length us, event | category | flops | bytes accessed | tf_op | source)
XLA Modules:
  0.0 457.0 jit_solution(7891196654021470663)
XLA Ops:
  8.3 4.5 while.49
  16.7 151.5 %all-gather.3.cloned.1.call-done = f32[32,1536,64]{1,2,0:T(8,128)} async-done(((f32[2,1536,64]{1,2,0:T(8,128)}), f32[32,1536,64]{1,2,0:T(8,128)}) %all-gather.3.cloned.1.call-update) | async-done | bytes 12582928 | tf_op jit(solution)/shard_map/all_gather | solution.py:126
  168.2 5.8 %reduce_sum.38 = f32[2,1536,64]{1,2,0:T(8,128)S(1)} reduce(f32[16,2,1536,64]{2,3,1,0:T(8,128)} %bitcast.97, f32[]{:T(128)} %constant.151.clone.1), dimensions={0}, to_apply=%region_4.0 | reduce | flops 2949120 | bytes 13369348 | tf_op jit(solution)/shard_map/reduce_sum | solution.py:126
  175.0 7.5 %all-to-all-start = ((f32[32,1,384]{2,1,0:T(1,128)}), f32[32,1,384]{2,1,0:T(1,128)S(1)}, u32[]{:S(2)}, u32[]{:S(2)}) async-start(f32[32,1,384]{2,1,0:T(1,128)} %reshape.73), calls=%async_computation | async-start | bytes 98304 | tf_op jit(solution)/shard_map/all_to_all | solution.py:130
  182.5 9.1 %all-to-all-done = f32[32,1,384]{2,1,0:T(1,128)S(1)} async-done(((f32[32,1,384]{2,1,0:T(1,128)}), f32[32,1,384]{2,1,0:T(1,128)S(1)}, u32[]{:S(2)}, u32[]{:S(2)}) %all-to-all-start) | async-done | bytes 49184 | tf_op jit(solution)/shard_map/all_to_all | solution.py:130
  193.5 176.8 %while.51 = (s32[]{:T(128)}, f32[24,4096]{1,0:T(8,128)S(1)}, s32[3,8,1]{1,0,2:T(4,128)}, s32[3,8,1]{1,0,2:T(4,128)}, bf16[24,4096]{1,0:T(8,128)(2,1)}, /*index=5...) while((s32[]{:T(128)}, f32[24,4096]{1,0:T(8,128)S(1)}, ...), condition=%wide.wide.region_6.7_spmd.clone, body=%wide.wide.region_5.6_spmd.clone.sunk | while | flops 118413576 | bytes 7291664 | solution.py:163
  193.5 8.6 %cosine_convert_fusion.3 = (bf16[2048,256]{1,0:T(8,128)(2,1)S(1)}, bf16[2048,256]{1,0:T(8,128)(2,1)S(1)}) fusion(s32[256]{0:T(256)S(1)} %iota_add_fusion.3), kind=kLoop, calls=%fused_computation.26.clone.clone.1 | loop fusion | flops 8912896 | bytes 2098176 | tf_op jit(solution)/shard_map/convert.1
  202.3 2.2 convolution_add_fusion.3
  204.5 8.6 %cosine_convert_fusion.3 = (bf16[2048,256]{1,0:T(8,128)(2,1)S(1)}, bf16[2048,256]{1,0:T(8,128)(2,1)S(1)}) fusion(s32[256]{0:T(256)S(1)} %iota_add_fusion.3), kind=kLoop, calls=%fused_computation.26.clone.clone.1 | loop fusion | flops 8912896 | bytes 2098176 | tf_op jit(solution)/shard_map/convert.1
  215.6 8.6 %cosine_convert_fusion.3 = (bf16[2048,256]{1,0:T(8,128)(2,1)S(1)}, bf16[2048,256]{1,0:T(8,128)(2,1)S(1)}) fusion(s32[256]{0:T(256)S(1)} %iota_add_fusion.3), kind=kLoop, calls=%fused_computation.26.clone.clone.1 | loop fusion | flops 8912896 | bytes 2098176 | tf_op jit(solution)/shard_map/convert.1
  224.4 2.2 convolution_add_fusion.3
  226.6 8.6 %cosine_convert_fusion.3 = (bf16[2048,256]{1,0:T(8,128)(2,1)S(1)}, bf16[2048,256]{1,0:T(8,128)(2,1)S(1)}) fusion(s32[256]{0:T(256)S(1)} %iota_add_fusion.3), kind=kLoop, calls=%fused_computation.26.clone.clone.1 | loop fusion | flops 8912896 | bytes 2098176 | tf_op jit(solution)/shard_map/convert.1
  237.7 8.6 %cosine_convert_fusion.3 = (bf16[2048,256]{1,0:T(8,128)(2,1)S(1)}, bf16[2048,256]{1,0:T(8,128)(2,1)S(1)}) fusion(s32[256]{0:T(256)S(1)} %iota_add_fusion.3), kind=kLoop, calls=%fused_computation.26.clone.clone.1 | loop fusion | flops 8912896 | bytes 2098176 | tf_op jit(solution)/shard_map/convert.1
  248.7 8.6 %cosine_convert_fusion.3 = (bf16[2048,256]{1,0:T(8,128)(2,1)S(1)}, bf16[2048,256]{1,0:T(8,128)(2,1)S(1)}) fusion(s32[256]{0:T(256)S(1)} %iota_add_fusion.3), kind=kLoop, calls=%fused_computation.26.clone.clone.1 | loop fusion | flops 8912896 | bytes 2098176 | tf_op jit(solution)/shard_map/convert.1
  257.5 2.2 convolution_add_fusion.3
  259.8 8.6 %cosine_convert_fusion.3 = (bf16[2048,256]{1,0:T(8,128)(2,1)S(1)}, bf16[2048,256]{1,0:T(8,128)(2,1)S(1)}) fusion(s32[256]{0:T(256)S(1)} %iota_add_fusion.3), kind=kLoop, calls=%fused_computation.26.clone.clone.1 | loop fusion | flops 8912896 | bytes 2098176 | tf_op jit(solution)/shard_map/convert.1
  270.8 8.6 %cosine_convert_fusion.3 = (bf16[2048,256]{1,0:T(8,128)(2,1)S(1)}, bf16[2048,256]{1,0:T(8,128)(2,1)S(1)}) fusion(s32[256]{0:T(256)S(1)} %iota_add_fusion.3), kind=kLoop, calls=%fused_computation.26.clone.clone.1 | loop fusion | flops 8912896 | bytes 2098176 | tf_op jit(solution)/shard_map/convert.1
  279.6 2.2 convolution_add_fusion.3
  281.9 8.6 %cosine_convert_fusion.3 = (bf16[2048,256]{1,0:T(8,128)(2,1)S(1)}, bf16[2048,256]{1,0:T(8,128)(2,1)S(1)}) fusion(s32[256]{0:T(256)S(1)} %iota_add_fusion.3), kind=kLoop, calls=%fused_computation.26.clone.clone.1 | loop fusion | flops 8912896 | bytes 2098176 | tf_op jit(solution)/shard_map/convert.1
  292.9 8.6 %cosine_convert_fusion.3 = (bf16[2048,256]{1,0:T(8,128)(2,1)S(1)}, bf16[2048,256]{1,0:T(8,128)(2,1)S(1)}) fusion(s32[256]{0:T(256)S(1)} %iota_add_fusion.3), kind=kLoop, calls=%fused_computation.26.clone.clone.1 | loop fusion | flops 8912896 | bytes 2098176 | tf_op jit(solution)/shard_map/convert.1
  304.0 8.6 %cosine_convert_fusion.3 = (bf16[2048,256]{1,0:T(8,128)(2,1)S(1)}, bf16[2048,256]{1,0:T(8,128)(2,1)S(1)}) fusion(s32[256]{0:T(256)S(1)} %iota_add_fusion.3), kind=kLoop, calls=%fused_computation.26.clone.clone.1 | loop fusion | flops 8912896 | bytes 2098176 | tf_op jit(solution)/shard_map/convert.1
  315.0 8.6 %cosine_convert_fusion.3 = (bf16[2048,256]{1,0:T(8,128)(2,1)S(1)}, bf16[2048,256]{1,0:T(8,128)(2,1)S(1)}) fusion(s32[256]{0:T(256)S(1)} %iota_add_fusion.3), kind=kLoop, calls=%fused_computation.26.clone.clone.1 | loop fusion | flops 8912896 | bytes 2098176 | tf_op jit(solution)/shard_map/convert.1
  326.1 8.6 %cosine_convert_fusion.3 = (bf16[2048,256]{1,0:T(8,128)(2,1)S(1)}, bf16[2048,256]{1,0:T(8,128)(2,1)S(1)}) fusion(s32[256]{0:T(256)S(1)} %iota_add_fusion.3), kind=kLoop, calls=%fused_computation.26.clone.clone.1 | loop fusion | flops 8912896 | bytes 2098176 | tf_op jit(solution)/shard_map/convert.1
  337.1 8.6 %cosine_convert_fusion.3 = (bf16[2048,256]{1,0:T(8,128)(2,1)S(1)}, bf16[2048,256]{1,0:T(8,128)(2,1)S(1)}) fusion(s32[256]{0:T(256)S(1)} %iota_add_fusion.3), kind=kLoop, calls=%fused_computation.26.clone.clone.1 | loop fusion | flops 8912896 | bytes 2098176 | tf_op jit(solution)/shard_map/convert.1
  348.2 8.6 %cosine_convert_fusion.3 = (bf16[2048,256]{1,0:T(8,128)(2,1)S(1)}, bf16[2048,256]{1,0:T(8,128)(2,1)S(1)}) fusion(s32[256]{0:T(256)S(1)} %iota_add_fusion.3), kind=kLoop, calls=%fused_computation.26.clone.clone.1 | loop fusion | flops 8912896 | bytes 2098176 | tf_op jit(solution)/shard_map/convert.1
  359.2 8.6 %cosine_convert_fusion.3 = (bf16[2048,256]{1,0:T(8,128)(2,1)S(1)}, bf16[2048,256]{1,0:T(8,128)(2,1)S(1)}) fusion(s32[256]{0:T(256)S(1)} %iota_add_fusion.3), kind=kLoop, calls=%fused_computation.26.clone.clone.1 | loop fusion | flops 8912896 | bytes 2098176 | tf_op jit(solution)/shard_map/convert.1
  371.6 3.6 reshape.75
  375.2 4.0 all-to-all-start.1
  379.3 8.9 %all-to-all-done.1 = f32[32,1,384]{2,1,0:T(1,128)S(1)} async-done(((f32[32,1,384]{2,1,0:T(1,128)}), f32[32,1,384]{2,1,0:T(1,128)S(1)}, u32[]{:S(2)}, u32[]{:S(2)}) %all-to-all-start.1) | async-done | bytes 49184 | tf_op jit(solution)/shard_map/all_to_all | solution.py:169
  389.0 3.1 reshape.76
  393.2 33.4 %all_gather.11 = f32[2,1536,64]{2,0,1:T(2,128)S(1)} all-gather(f32[2,96,64]{2,0,1:T(2,128)S(1)} %bitcast.111), channel_id=1, replica_groups=mesh['pair'=32,'day'=16] {'day'}, dimensions={1}, use_global_device_ids=true | all-gather | bytes 835584 | tf_op jit(solution)/shard_map/all_gather | solution.py:171
  436.7 12.5 %while.50 = (s32[]{:T(128)}, f32[256,1024]{1,0:T(8,128)S(1)}, f32[256,1536]{1,0:T(8,128)}, f32[256,1536]{1,0:T(8,128)}, s32[1536,2]{0,1:T(2,128)S(1)}, /*index=5...) while((s32[]{:T(128)}, f32[256,1024]{1,0:T(8,128)S(1)}, f32[256,1536]{1,0:T(8,128)}, ...), condition=%wide.region_9.10_spmd.clone.clone, body=%wide.region_8.9_spmd.clone.clone.sunk | while | flops 3224109056 | bytes 7352501 | solution.py:83
  (157 shorter events, 68.0 us)
Async XLA Ops:
  6.5 1.8 copy-start.8
  6.5 161.6 %all-gather.3.cloned.1.call-start = ((), (), s32[]{:S(2)}) async-start(), calls=%async_computation.2 | async-start | bytes 13369344 | tf_op jit(solution)/shard_map/all_gather | solution.py:126
  13.2 1.2 copy-start
  13.2 1.7 copy-start.2
  14.8 1.0 copy-start.7
  14.8 1.8 copy-start.4
  15.8 158.2 %copy-start.5 = (s32[3,8,1]{1,0,2:T(4,128)}, s32[3,8,1]{1,0,2:T(4,128)S(1)}, u32[]{:S(2)}) copy-start(s32[3,8,1]{1,0,2:T(4,128)S(1)} %copy.86) | copy-start | bytes 292
  15.9 158.1 %copy-start.6 = (s32[3,8,1]{1,0,2:T(4,128)}, s32[3,8,1]{1,0,2:T(4,128)S(1)}, u32[]{:S(2)}) copy-start(s32[3,8,1]{1,0,2:T(4,128)S(1)} %copy.87) | copy-start | bytes 292
  175.0 16.6 %all-to-all-start = ((f32[32,1,384]{2,1,0:T(1,128)}), f32[32,1,384]{2,1,0:T(1,128)S(1)}, u32[]{:S(2)}, u32[]{:S(2)}) async-start(f32[32,1,384]{2,1,0:T(1,128)} %reshape.73), calls=%async_computation | async-start | bytes 98304 | tf_op jit(solution)/shard_map/all_to_all | solution.py:130
  375.2 12.9 %all-to-all-start.1 = ((f32[32,1,384]{2,1,0:T(1,128)}), f32[32,1,384]{2,1,0:T(1,128)S(1)}, u32[]{:S(2)}, u32[]{:S(2)}) async-start(f32[32,1,384]{2,1,0:T(1,128)} %reshape.75), calls=%async_computation.1 | async-start | bytes 98304 | tf_op jit(solution)/shard_map/all_to_all | solution.py:169
  426.6 5.7 %copy-start.1 = (f32[2,2,64,1536]{3,2,1,0:T(8,128)S(1)}, f32[2,2,64,1536]{3,2,1,0:T(8,128)}, u32[]{:S(2)}) copy-start(f32[2,2,64,1536]{3,2,1,0:T(8,128)} %copy-done) | copy-start | bytes 4718596
  426.6 5.7 %copy-start.3 = (f32[2,2,64,1536]{3,2,1,0:T(8,128)S(1)}, f32[2,2,64,1536]{3,2,1,0:T(8,128)}, u32[]{:S(2)}) copy-start(f32[2,2,64,1536]{3,2,1,0:T(8,128)} %copy-done.2) | copy-start | bytes 4718596
  435.0 1.7 copy-start.9
  449.2 1.0 copy-start.10
Sparse Core Ops, SparseCore 0:
  15.9 152.2 all-gather.2
